TPU v7x, 32 devices: a whole 2x2x4 slice. The times are simulated.
32 devices in a mesh: sh: 4 (over z), sw: 4 (over y, core), tp: 2 (over x).
Axes of the slice: x: 2, y: 2, z: 4, core: 2. Of those that a mesh axis runs over, the one named last changes fastest.
Arguments:
- queries: bfloat16 [2, 32, 32, 1536], P('tp', 'sh', 'sw'), may hold values from -6 to 6
- keys: bfloat16 [2, 32, 32, 1536], P('tp', 'sh', 'sw'), may hold values from -6 to 6
- values: bfloat16 [2, 32, 32, 1536], P('tp', 'sh', 'sw'), may hold values from -6 to 6
- attn_out: bfloat16 [2, 32, 32, 1536], P('tp', 'sh', 'sw'), may hold values from -6 to 6
- attn_grad: bfloat16 [2, 32, 32, 1536], P('tp', 'sh', 'sw'), may hold values from -192 to 192
- log_sum: float32 [2, 32, 32, 12], P('tp', 'sh', 'sw'), may hold values from 6.1 to 6.9
- window_dirs: int32 [12, 4], replicated, may hold values from 0 to 7, as said below
Outputs:
- q_grad: bfloat16 [2, 32, 32, 1536], P('tp', 'sh', 'sw')
- k_grad: bfloat16 [2, 32, 32, 1536], P('tp', 'sh', 'sw')
- v_grad: bfloat16 [2, 32, 32, 1536], P('tp', 'sh', 'sw')
Inputs may be any that keep to these rules, and one draw needn't show every extreme that they name: `window_dirs`: each row names 4 different directions. Within each run of 6 consecutive heads (those of one index of tp) every direction is named by exactly half of the rows.
All inputs are finite; a program needn't handle non-finite values.
Results may differ from a plain program's by a relative error of at most 0.0056.
Values may be sent and summed in bfloat16 or wider, within the bound.
A program may use at most 64 MiB of HBM per device.

v0:
```python
import jax
import jax.numpy as jnp
from jax import lax
from jax.sharding import PartitionSpec as P

NEIGHBOURS = ((-1, -1), (-1, 0), (-1, 1), (0, -1), (0, 1), (1, -1), (1, 0), (1, 1))


def passed_along(block, axis, distance):
    devices = range(lax.axis_size(axis))
    route = [(i - distance, i) for i in devices if i - distance in devices]
    return lax.ppermute(block, axis, route)


def slot_tables(local_dirs):
    head_count = local_dirs.shape[0]
    half_heads = head_count // 2
    directions = jnp.arange(8, dtype=jnp.int32)
    listed = (local_dirs[:, :, None] == directions[None, None, :]).astype(jnp.int32)
    member = jnp.sum(listed, axis=1)
    position = jnp.sum(listed * jnp.arange(4, dtype=jnp.int32)[None, :, None], axis=1)
    rank_in = jnp.cumsum(member, axis=0) - 1
    slot_of = jnp.sum(listed * rank_in[:, None, :], axis=2)
    chosen = member[:, :, None] * (
        rank_in[:, :, None] == jnp.arange(half_heads, dtype=jnp.int32)[None, None, :]
    ).astype(jnp.int32)
    head_ids = jnp.arange(head_count, dtype=jnp.int32)
    head_of = jnp.sum(chosen * head_ids[:, None, None], axis=0)
    place_of = jnp.sum(chosen * position[:, :, None], axis=0)
    return (slot_of, head_of, place_of)


def bounds(offsets, direction_sign):
    grid_row = lax.axis_index("sh")
    grid_col = lax.axis_index("sw")
    target_row = grid_row + direction_sign * offsets[:, 0]
    target_col = grid_col + direction_sign * offsets[:, 1]
    inside = (
        (target_row >= 0)
        & (target_row < lax.axis_size("sh"))
        & (target_col >= 0)
        & (target_col < lax.axis_size("sw"))
    )
    return inside.astype(jnp.float32)


def pull_blocks(packs):
    arrived = {}
    for step_row in (-1, 1):
        stacked = jnp.stack(
            [packs[NEIGHBOURS.index((step_row, step_col))] for step_col in (-1, 0, 1)]
        )
        arrived[step_row] = passed_along(stacked, "sh", -step_row)
    result = {}
    for step_row in (-1, 1):
        result[step_row, 0] = arrived[step_row][1]
    for step_col in (-1, 1):
        column_pick = 0 if step_col < 0 else 2
        stacked = jnp.stack(
            [
                arrived[-1][column_pick],
                packs[NEIGHBOURS.index((0, step_col))],
                arrived[1][column_pick],
            ]
        )
        shifted = passed_along(stacked, "sw", -step_col)
        result[-1, step_col] = shifted[0]
        result[0, step_col] = shifted[1]
        result[1, step_col] = shifted[2]
    return jnp.stack([result[offset_pair] for offset_pair in NEIGHBOURS])


def send_out(packs, along_cols, along_rows):
    arrived = {}
    for step_col in (-1, 1):
        stacked = jnp.stack(
            [packs[NEIGHBOURS.index((step_row, step_col))] for step_row in (-1, 0, 1)]
        )
        arrived[step_col] = along_cols(stacked, step_col)
    result = {}
    for step_col in (-1, 1):
        result[0, step_col] = arrived[step_col][1]
    for step_row in (-1, 1):
        row_pick = 0 if step_row < 0 else 2
        stacked = jnp.stack(
            [arrived[-1][row_pick], packs[NEIGHBOURS.index((step_row, 0))], arrived[1][row_pick]]
        )
        shifted = along_rows(stacked, step_row)
        result[step_row, -1] = shifted[0]
        result[step_row, 0] = shifted[1]
        result[step_row, 1] = shifted[2]
    return jnp.stack([result[offset_pair] for offset_pair in NEIGHBOURS])


def local(queries, keys, values, attn_out, attn_grad, log_sum, window_dirs):
    frames_here, tile_rows, tile_cols, width_all = queries.shape
    head_total = log_sum.shape[3]
    head_dim = width_all // head_total
    row_delta = jnp.sum(
        (attn_grad.astype(jnp.float32) * attn_out.astype(jnp.float32)).reshape(
            frames_here, tile_rows, tile_cols, head_total, head_dim
        ),
        axis=4,
    )
    q_heads, k_heads, v_heads, g_heads = (
        lax.all_to_all(queries, "tp", split_axis=3, concat_axis=0, tiled=True),
        lax.all_to_all(keys, "tp", split_axis=3, concat_axis=0, tiled=True),
        lax.all_to_all(values, "tp", split_axis=3, concat_axis=0, tiled=True),
        lax.all_to_all(attn_grad, "tp", split_axis=3, concat_axis=0, tiled=True),
    )
    lse_heads, delta_heads = (
        lax.all_to_all(log_sum, "tp", split_axis=3, concat_axis=0, tiled=True),
        lax.all_to_all(row_delta, "tp", split_axis=3, concat_axis=0, tiled=True),
    )
    frames_all = q_heads.shape[0]
    head_here = q_heads.shape[3] // head_dim
    tile_tok = frames_all * tile_rows * tile_cols
    score_scale = head_dim ** (-0.5)

    def by_head(array):
        return jnp.transpose(array.reshape(tile_tok, head_here, head_dim), (1, 0, 2))

    q_own = by_head(q_heads)
    k_own = by_head(k_heads)
    v_own = by_head(v_heads)
    g_own = by_head(g_heads)
    lse_own = lse_heads.reshape(tile_tok, head_here).T
    delta_own = delta_heads.reshape(tile_tok, head_here).T
    local_dirs = lax.dynamic_slice_in_dim(
        window_dirs, lax.axis_index("tp") * head_here, head_here, 0
    )
    slot_of, head_of, place_of = slot_tables(local_dirs)
    offsets = jnp.array(NEIGHBOURS, dtype=jnp.int32)
    ahead_live = bounds(offsets, 1)
    kv_own = jnp.stack([k_own, v_own], axis=1)
    kv_packs = [jnp.take(kv_own, head_of[direction], axis=0) for direction in range(8)]
    recv_kv = pull_blocks(kv_packs)
    nb_kv = recv_kv[local_dirs, slot_of]
    k_all = jnp.concatenate([k_own[:, None], nb_kv[:, :, 0]], axis=1).reshape(
        head_here, 5 * tile_tok, head_dim
    )
    v_all = jnp.concatenate([v_own[:, None], nb_kv[:, :, 1]], axis=1).reshape(
        head_here, 5 * tile_tok, head_dim
    )
    live_all = jnp.concatenate(
        [
            jnp.ones((head_here, tile_tok), jnp.float32),
            jnp.repeat(ahead_live[local_dirs], tile_tok, axis=1),
        ],
        axis=1,
    )
    key_count = 5 * tile_tok
    contract_rows = (((0,), (0,)), ((), ()))
    contract_cols = (((1,), (1,)), ((), ()))

    def query_side(inputs):
        q_rows, g_rows, lse_row, delta_row, k_rows, v_rows, live_row = inputs
        scores = (
            lax.dot_general(q_rows, k_rows, contract_cols, preferred_element_type=jnp.float32)
            * score_scale
        )
        attn_prob = jnp.exp(scores - lse_row[:, None]) * live_row[None, :]
        grad_prob = lax.dot_general(
            g_rows, v_rows, contract_cols, preferred_element_type=jnp.float32
        )
        grad_score = attn_prob * (grad_prob - delta_row[:, None])
        score_bf = grad_score.astype(jnp.bfloat16)
        prob_bf = attn_prob.astype(jnp.bfloat16)
        q_grad = jnp.dot(score_bf, k_rows, preferred_element_type=jnp.float32) * score_scale
        k_part = (
            lax.dot_general(score_bf, q_rows, contract_rows, preferred_element_type=jnp.float32)
            * score_scale
        )
        v_part = lax.dot_general(prob_bf, g_rows, contract_rows, preferred_element_type=jnp.float32)
        return (q_grad, k_part, v_part)

    q_grad, k_part, v_part = lax.map(
        query_side, (q_own, g_own, lse_own, delta_own, k_all, v_all, live_all)
    )
    k_self = k_part[:, :tile_tok]
    v_self = v_part[:, :tile_tok]
    part_bf = jnp.stack(
        [
            k_part[:, tile_tok:].reshape(head_here, 4, tile_tok, head_dim),
            v_part[:, tile_tok:].reshape(head_here, 4, tile_tok, head_dim),
        ],
        axis=2,
    ).astype(jnp.bfloat16)
    part_packs = [part_bf[head_of[direction], place_of[direction]] for direction in range(8)]
    returned = send_out(
        part_packs,
        lambda moving, offset_step: passed_along(moving, "sw", offset_step),
        lambda moving, offset_step: passed_along(moving, "sh", offset_step),
    )
    mine_parts = returned[local_dirs, slot_of]
    summed = jnp.sum(mine_parts.astype(jnp.float32), axis=1)
    k_total = k_self + summed[:, 0]
    v_total = v_self + summed[:, 1]

    def by_token(array):
        return jnp.transpose(array.astype(jnp.bfloat16), (1, 0, 2)).reshape(
            frames_all, tile_rows, tile_cols, head_here * head_dim
        )

    return (
        lax.all_to_all(by_token(q_grad), "tp", split_axis=0, concat_axis=3, tiled=True),
        lax.all_to_all(by_token(k_total), "tp", split_axis=0, concat_axis=3, tiled=True),
        lax.all_to_all(by_token(v_total), "tp", split_axis=0, concat_axis=3, tiled=True),
    )


def solution(mesh):
    return jax.shard_map(
        local,
        mesh=mesh,
        in_specs=(
            P("tp", "sh", "sw", None),
            P("tp", "sh", "sw", None),
            P("tp", "sh", "sw", None),
            P("tp", "sh", "sw", None),
            P("tp", "sh", "sw", None),
            P("tp", "sh", "sw", None),
            P(),
        ),
        out_specs=(P("tp", "sh", "sw", None), P("tp", "sh", "sw", None), P("tp", "sh", "sw", None)),
        check_vma=False,
    )
```

profile of v0, /device:TPU:4, one launch (start us, length us, event | category | flops | bytes accessed | tf_op | source)
XLA Modules:
  0.0 248.6 jit_solution(4305474917567733513)
XLA Ops:
  0.6 3.2 %copy.106 = bf16[1,8,8,1536]{2,1,0,3:T(8,128)(2,1)S(1)} copy(bf16[1,8,8,1536]{3,2,1,0:T(8,128)(2,1)} %param.13) | data formatting | bytes 393216 | tf_op args[1]
  3.8 4.1 %reshape.753 = bf16[2,2,24576]{2,1,0:T(2,128)(2,1)} reshape(bf16[1536,1,8,8]{3,2,1,0:T(8,128)(2,1)S(1)} %bitcast.299) | data formatting | bytes 393216
  7.9 3.4 %all-to-all-start.1 = ((bf16[2,2,24576]{2,1,0:T(2,128)(2,1)}), bf16[2,2,24576]{2,1,0:T(2,128)(2,1)S(1)}, u32[]{:S(2)}, u32[]{:S(2)}) async-start(bf16[2,2,24576]{2,1,0:T(2,128)(2,1)} %reshape.753), calls=%async_computation.1 | async-start | bytes 393216 | tf_op jit(solution)/shard_map/all_to_all | solution.py:107
  24.6 2.2 copy.110
  26.8 4.1 %reshape.751 = bf16[2,2,24576]{2,1,0:T(2,128)(2,1)} reshape(bf16[1536,1,8,8]{3,2,1,0:T(8,128)(2,1)S(1)} %bitcast.300) | data formatting | bytes 393216
  30.9 4.1 %all-to-all-start.2 = ((bf16[2,2,24576]{2,1,0:T(2,128)(2,1)}), bf16[2,2,24576]{2,1,0:T(2,128)(2,1)}, u32[]{:S(2)}, u32[]{:S(2)}) async-start(bf16[2,2,24576]{2,1,0:T(2,128)(2,1)} %reshape.751), calls=%async_computation.2 | async-start | bytes 393216 | tf_op jit(solution)/shard_map/all_to_all | solution.py:108
  35.1 3.7 %reshape.754 = bf16[1536,1,8,8]{3,2,1,0:T(8,128)(2,1)S(1)} reshape(bf16[2,2,24576]{2,1,0:T(2,128)(2,1)S(1)} %all-to-all-done.1) | data formatting | bytes 393216
  38.7 2.4 copy.107
  42.3 3.3 %all-to-all-start.3 = ((f32[2,1,384]{2,1,0:T(1,128)}), f32[2,1,384]{2,1,0:T(1,128)S(1)}, u32[]{:S(2)}, u32[]{:S(2)}) async-start(f32[2,1,384]{2,1,0:T(1,128)} %reshape.755), calls=%async_computation.3 | async-start | bytes 6144 | tf_op jit(solution)/shard_map/all_to_all | solution.py:112
  45.6 4.5 %reshape.752 = bf16[1536,1,8,8]{3,2,1,0:T(8,128)(2,1)S(1)} reshape(bf16[2,2,24576]{2,1,0:T(2,128)(2,1)} %all-to-all-done.2) | data formatting | bytes 393216
  50.1 2.4 copy.111
  58.3 3.6 %collective-permute-start = (bf16[3,3,2,128,128]{4,3,2,1,0:T(8,128)(2,1)S(1)}, bf16[3,3,2,128,128]{4,3,2,1,0:T(8,128)(2,1)S(1)}, u32[]{:S(2)}, u32[]{:S(2)}) collective-permute-start(bf16[3,3,2,128,128]{4,3,2,1,0:T(8,128)(2,1)S(1)} %pad_maximum_fusion.4), channel_id=1, source_target_pairs={{0,8},{8,16},{16,24},{1,9},{9,17},{17,25},{2,10},{10,18},{18,26},{... | collective-permute-start | bytes 1769480 | tf_op jit(solution)/shard_map/ppermute | solution.py:12
  62.3 1.3 collective-permute-start.1
  65.1 9.3 %collective-permute-done = bf16[3,3,2,128,128]{4,3,2,1,0:T(8,128)(2,1)S(1)} collective-permute-done((bf16[3,3,2,128,128]{4,3,2,1,0:T(8,128)(2,1)S(1)}, bf16[3,3,2,128,128]{4,3,2,1,0:T(8,128)(2,1)S(1)}, u32[]{:S(2)}, u32[]{:S(2)}) %collective-permute-start) | collective-permute-done | bytes 589856 | tf_op jit(solution)/shard_map/ppermute | solution.py:12
  74.4 4.5 %collective-permute-done.1 = bf16[3,3,2,128,128]{4,3,2,1,0:T(8,128)(2,1)S(1)} collective-permute-done((bf16[3,3,2,128,128]{4,3,2,1,0:T(8,128)(2,1)S(1)}, bf16[3,3,2,128,128]{4,3,2,1,0:T(8,128)(2,1)S(1)}, u32[]{:S(2)}, u32[]{:S(2)}) %collective-permute-start.1) | collective-permute-done | bytes 589856 | tf_op jit(solution)/shard_map/ppermute | solution.py:12
  79.0 1.9 collective-permute-start.2
  83.3 7.0 %collective-permute-done.2 = bf16[3,3,2,128,128]{4,3,2,1,0:T(8,128)(2,1)S(1)} collective-permute-done((bf16[3,3,2,128,128]{4,3,2,1,0:T(8,128)(2,1)S(1)}, bf16[3,3,2,128,128]{4,3,2,1,0:T(8,128)(2,1)S(1)}, u32[]{:S(2)}, u32[]{:S(2)}) %collective-permute-start.2) | collective-permute-done | bytes 589856 | tf_op jit(solution)/shard_map/ppermute | solution.py:12
  92.5 1.9 collective-permute-start.3
  94.5 3.4 %all-to-all-start.5 = ((f32[2,1,384]{2,1,0:T(1,128)}), f32[2,1,384]{2,1,0:T(1,128)S(1)}, u32[]{:S(2)}, u32[]{:S(2)}) async-start(f32[2,1,384]{2,1,0:T(1,128)} %reshape.759), calls=%async_computation.5 | async-start | bytes 6144 | tf_op jit(solution)/shard_map/all_to_all | solution.py:113
  98.4 3.1 %copy.104 = bf16[1,8,8,1536]{2,1,0,3:T(8,128)(2,1)S(1)} copy(bf16[1,8,8,1536]{3,2,1,0:T(8,128)(2,1)} %param.12) | data formatting | bytes 393216 | tf_op args[0]
  101.6 4.2 %reshape.749 = bf16[2,2,24576]{2,1,0:T(2,128)(2,1)} reshape(bf16[1536,1,8,8]{3,2,1,0:T(8,128)(2,1)S(1)} %bitcast.301) | data formatting | bytes 393216
  105.8 4.1 %all-to-all-start = ((bf16[2,2,24576]{2,1,0:T(2,128)(2,1)}), bf16[2,2,24576]{2,1,0:T(2,128)(2,1)}, u32[]{:S(2)}, u32[]{:S(2)}) async-start(bf16[2,2,24576]{2,1,0:T(2,128)(2,1)} %reshape.749), calls=%async_computation | async-start | bytes 393216 | tf_op jit(solution)/shard_map/all_to_all | solution.py:106
  109.9 1.3 fusion.91
  111.2 3.1 %copy.118 = bf16[1,8,8,1536]{2,1,0,3:T(8,128)(2,1)S(1)} copy(bf16[1,8,8,1536]{3,2,1,0:T(8,128)(2,1)} %param.16) | data formatting | bytes 393216 | tf_op args[4]
  114.3 4.2 %reshape.757 = bf16[2,2,24576]{2,1,0:T(2,128)(2,1)} reshape(bf16[1536,1,8,8]{3,2,1,0:T(8,128)(2,1)S(1)} %bitcast.302) | data formatting | bytes 393216
  118.6 4.1 %all-to-all-start.4 = ((bf16[2,2,24576]{2,1,0:T(2,128)(2,1)}), bf16[2,2,24576]{2,1,0:T(2,128)(2,1)}, u32[]{:S(2)}, u32[]{:S(2)}) async-start(bf16[2,2,24576]{2,1,0:T(2,128)(2,1)} %reshape.757), calls=%async_computation.4 | async-start | bytes 393216 | tf_op jit(solution)/shard_map/all_to_all | solution.py:109
  122.7 1.3 fusion.92
  125.2 1.3 reduce.43
  126.8 1.3 reduce.44
  128.3 4.5 %reshape.750 = bf16[1536,1,8,8]{3,2,1,0:T(8,128)(2,1)S(1)} reshape(bf16[2,2,24576]{2,1,0:T(2,128)(2,1)} %all-to-all-done) | data formatting | bytes 393216
  132.8 2.4 copy.105
  135.2 1.2 reshape.545
  137.1 4.5 %reshape.758 = bf16[1536,1,8,8]{3,2,1,0:T(8,128)(2,1)S(1)} reshape(bf16[2,2,24576]{2,1,0:T(2,128)(2,1)} %all-to-all-done.4) | data formatting | bytes 393216
  141.6 2.4 copy.119
  145.2 1.6 slice_dynamic-update-slice_fusion.5
  146.8 1.6 slice_dynamic-update-slice_fusion.4
  148.4 1.6 slice_dynamic-update-slice_fusion.3
  150.1 1.6 slice_dynamic-update-slice_fusion.2
  151.7 1.6 slice_dynamic-update-slice_fusion.1
  153.3 1.6 slice_dynamic-update-slice_fusion
  154.9 2.3 gather_fusion
  158.3 29.2 %while.14 = (s32[]{:T(128)}, bf16[6,128,128]{2,1,0:T(8,128)(2,1)S(1)}, f32[6,640,128]{2,1,0:T(8,128)}, f32[6,640,128]{2,1,0:T(8,128)}, bf16[6,128,128]{2,1,0:T(8...) while((s32[]{:T(128)}, ...), condition=%wide.region_6.8_spmd, body=%wide.region_5.7_spmd.sunk | while | flops 105529344 | bytes 2835589 | solution.py:177
  161.4 1.7 fusion.131
  166.3 1.7 fusion.131
  171.1 1.7 fusion.131
  176.0 1.7 fusion.131
  180.9 1.7 fusion.131
  185.8 1.7 fusion.131
  187.5 1.5 slice.304
  189.0 1.5 slice.305
  193.0 1.9 collective-permute-start.4
  198.3 2.8 %collective-permute-start.5 = (bf16[3,3,2,128,128]{4,3,2,1,0:T(8,128)(2,1)}, bf16[3,3,2,128,128]{4,3,2,1,0:T(8,128)(2,1)}, u32[]{:S(2)}, u32[]{:S(2)}) collective-permute-start(bf16[3,3,2,128,128]{4,3,2,1,0:T(8,128)(2,1)} %pad_maximum_fusion.9), channel_id=1, source_target_pairs={{0,2},{2,4},{4,6},{1,3},{3,5},{5,7},{8,10},{10,12},{12,14},{9,11},... | collective-permute-start | bytes 1769480 | tf_op jit(solution)/shard_map/ppermute | solution.py:12
  203.7 6.1 %collective-permute-done.5 = bf16[3,3,2,128,128]{4,3,2,1,0:T(8,128)(2,1)} collective-permute-done((bf16[3,3,2,128,128]{4,3,2,1,0:T(8,128)(2,1)}, bf16[3,3,2,128,128]{4,3,2,1,0:T(8,128)(2,1)}, u32[]{:S(2)}, u32[]{:S(2)}) %collective-permute-start.5) | collective-permute-done | bytes 589856 | tf_op jit(solution)/shard_map/ppermute | solution.py:12
  211.0 3.5 %collective-permute-start.7 = (bf16[3,3,2,128,128]{4,3,2,1,0:T(8,128)(2,1)S(1)}, bf16[3,3,2,128,128]{4,3,2,1,0:T(8,128)(2,1)S(1)}, u32[]{:S(2)}, u32[]{:S(2)}) collective-permute-start(bf16[3,3,2,128,128]{4,3,2,1,0:T(8,128)(2,1)S(1)} %pad_maximum_fusion.11), channel_id=1, source_target_pairs={{0,8},{8,16},{16,24},{1,9},{9,17},{17,25},{2,10},{10,18},{18,26},{... | collective-permute-start | bytes 1769480 | tf_op jit(solution)/shard_map/ppermute | solution.py:12
  214.6 1.3 collective-permute-start.6
  217.0 3.4 %all-to-all-start.6 = ((bf16[2,8,8,768]{3,2,1,0:T(8,128)(2,1)}), bf16[2,8,8,768]{3,2,1,0:T(8,128)(2,1)S(1)}, u32[]{:S(2)}, u32[]{:S(2)}) async-start(bf16[2,8,8,768]{3,2,1,0:T(8,128)(2,1)} %reshape.555), calls=%async_computation.6 | async-start | bytes 393216 | tf_op jit(solution)/shard_map/all_to_all | solution.py:206
  220.4 1.5 collective-permute-done.7
  221.9 4.6 %collective-permute-done.6 = bf16[3,3,2,128,128]{4,3,2,1,0:T(8,128)(2,1)} collective-permute-done((bf16[3,3,2,128,128]{4,3,2,1,0:T(8,128)(2,1)S(1)}, bf16[3,3,2,128,128]{4,3,2,1,0:T(8,128)(2,1)}, u32[]{:S(2)}, u32[]{:S(2)}) %collective-permute-start.6) | collective-permute-done | bytes 589856 | tf_op jit(solution)/shard_map/ppermute | solution.py:12
  226.5 1.4 pad_maximum_fusion.1
  229.1 1.2 fusion.38
  231.4 3.4 %all-to-all-start.8 = ((bf16[2,8,8,768]{3,2,1,0:T(8,128)(2,1)}), bf16[2,8,8,768]{3,2,1,0:T(8,128)(2,1)S(1)}, u32[]{:S(2)}, u32[]{:S(2)}) async-start(bf16[2,8,8,768]{3,2,1,0:T(8,128)(2,1)} %reshape.557), calls=%async_computation.8 | async-start | bytes 393216 | tf_op jit(solution)/shard_map/all_to_all | solution.py:208
  235.9 3.7 %all-to-all-done.8 = bf16[2,8,8,768]{3,2,1,0:T(8,128)(2,1)S(1)} async-done(((bf16[2,8,8,768]{3,2,1,0:T(8,128)(2,1)}), bf16[2,8,8,768]{3,2,1,0:T(8,128)(2,1)S(1)}, u32[]{:S(2)}, u32[]{:S(2)}) %all-to-all-start.8) | async-done | bytes 196640 | tf_op jit(solution)/shard_map/all_to_all | solution.py:208
  239.7 3.4 %all-to-all-start.7 = ((bf16[2,8,8,768]{3,2,1,0:T(8,128)(2,1)}), bf16[2,8,8,768]{3,2,1,0:T(8,128)(2,1)S(1)}, u32[]{:S(2)}, u32[]{:S(2)}) async-start(bf16[2,8,8,768]{3,2,1,0:T(8,128)(2,1)} %reshape.556), calls=%async_computation.7 | async-start | bytes 393216 | tf_op jit(solution)/shard_map/all_to_all | solution.py:207
  244.5 3.4 %all-to-all-done.7 = bf16[2,8,8,768]{3,2,1,0:T(8,128)(2,1)S(1)} async-done(((bf16[2,8,8,768]{3,2,1,0:T(8,128)(2,1)}), bf16[2,8,8,768]{3,2,1,0:T(8,128)(2,1)S(1)}, u32[]{:S(2)}, u32[]{:S(2)}) %all-to-all-start.7) | async-done | bytes 196640 | tf_op jit(solution)/shard_map/all_to_all | solution.py:207
  (247 shorter events, 66.3 us)
Async XLA Ops:
  3.8 7.5 %copy-start.16 = (s32[12,4]{0,1:T(4,128)S(1)}, s32[12,4]{0,1:T(4,128)}, u32[]{:S(2)}) copy-start(s32[12,4]{0,1:T(4,128)} %param.18) | copy-start | bytes 580
  3.8 20.8 %copy-start.4 = (bf16[1,8,8,1536]{3,2,1,0:T(8,128)(2,1)S(1)}, bf16[1,8,8,1536]{3,2,1,0:T(8,128)(2,1)}, u32[]{:S(2)}) copy-start(bf16[1,8,8,1536]{3,2,1,0:T(8,128)(2,1)} %param.14) | copy-start | bytes 589828
  7.9 23.1 %all-to-all-start.1 = ((bf16[2,2,24576]{2,1,0:T(2,128)(2,1)}), bf16[2,2,24576]{2,1,0:T(2,128)(2,1)S(1)}, u32[]{:S(2)}, u32[]{:S(2)}) async-start(bf16[2,2,24576]{2,1,0:T(2,128)(2,1)} %reshape.753), calls=%async_computation.1 | async-start | bytes 393216 | tf_op jit(solution)/shard_map/all_to_all | solution.py:107
  12.8 9.5 %copy-start.17 = (s32[3]{0:T(128)}, s32[3]{0:T(128)S(1)}, u32[]{:S(2)}) copy-start(s32[3]{0:T(128)S(1)} %get-tuple-element.188) | copy-start | bytes 40
  12.8 9.5 %copy-start.18 = (s32[3]{0:T(128)}, s32[3]{0:T(128)S(1)}, u32[]{:S(2)}) copy-start(s32[3]{0:T(128)S(1)} %get-tuple-element.184) | copy-start | bytes 40
  12.8 9.5 %copy-start.19 = (s32[3]{0:T(128)}, s32[3]{0:T(128)S(1)}, u32[]{:S(2)}) copy-start(s32[3]{0:T(128)S(1)} %get-tuple-element.185) | copy-start | bytes 40
  12.8 9.5 %copy-start.20 = (s32[3]{0:T(128)}, s32[3]{0:T(128)S(1)}, u32[]{:S(2)}) copy-start(s32[3]{0:T(128)S(1)} %get-tuple-element.183) | copy-start | bytes 40
  12.8 9.5 %copy-start.21 = (s32[3]{0:T(128)}, s32[3]{0:T(128)S(1)}, u32[]{:S(2)}) copy-start(s32[3]{0:T(128)S(1)} %get-tuple-element.186) | copy-start | bytes 40
  12.8 9.6 %copy-start.23 = (s32[3]{0:T(128)}, s32[3]{0:T(128)S(1)}, u32[]{:S(2)}) copy-start(s32[3]{0:T(128)S(1)} %get-tuple-element.187) | copy-start | bytes 40
  26.8 4.1 %copy-start.34 = (s32[8,1]{0,1:T(1,128)S(1)}, s32[8,1]{0,1:T(1,128)}, u32[]{:S(2)}) copy-start(s32[8,1]{0,1:T(1,128)} %constant.90) | copy-start | bytes 100
  26.8 4.1 %copy-start.35 = (s32[8,1]{0,1:T(1,128)S(1)}, s32[8,1]{0,1:T(1,128)}, u32[]{:S(2)}) copy-start(s32[8,1]{0,1:T(1,128)} %constant.89) | copy-start | bytes 100
  26.8 4.1 %copy-start.37 = (s32[3]{0:T(128)S(1)}, s32[3]{0:T(128)}, u32[]{:S(2)}) copy-start(s32[3]{0:T(128)} %compare_select_fusion.8) | copy-start | bytes 40
  26.8 8.2 %copy-start.36 = (s32[3]{0:T(128)S(1)}, s32[3]{0:T(128)}, u32[]{:S(2)}) copy-start(s32[3]{0:T(128)} %compare_select_fusion.9) | copy-start | bytes 40
  30.9 11.3 %all-to-all-start.2 = ((bf16[2,2,24576]{2,1,0:T(2,128)(2,1)}), bf16[2,2,24576]{2,1,0:T(2,128)(2,1)}, u32[]{:S(2)}, u32[]{:S(2)}) async-start(bf16[2,2,24576]{2,1,0:T(2,128)(2,1)} %reshape.751), calls=%async_computation.2 | async-start | bytes 393216 | tf_op jit(solution)/shard_map/all_to_all | solution.py:108
  42.3 52.1 %all-to-all-start.3 = ((f32[2,1,384]{2,1,0:T(1,128)}), f32[2,1,384]{2,1,0:T(1,128)S(1)}, u32[]{:S(2)}, u32[]{:S(2)}) async-start(f32[2,1,384]{2,1,0:T(1,128)} %reshape.755), calls=%async_computation.3 | async-start | bytes 6144 | tf_op jit(solution)/shard_map/all_to_all | solution.py:112
  53.7 4.1 %copy-start.32 = (pred[3]{0:T(512)(128)(4,1)S(1)}, pred[3]{0:T(512)(128)(4,1)}, u32[]{:S(2)}) copy-start(pred[3]{0:T(512)(128)(4,1)} %compare_and_fusion.5) | copy-start | bytes 13
  53.8 4.2 %copy-start.31 = (pred[3]{0:T(512)(128)(4,1)S(1)}, pred[3]{0:T(512)(128)(4,1)}, u32[]{:S(2)}) copy-start(pred[3]{0:T(512)(128)(4,1)} %compare_and_fusion.7) | copy-start | bytes 13
  53.8 4.3 %copy-start.30 = (pred[3]{0:T(512)(128)(4,1)S(1)}, pred[3]{0:T(512)(128)(4,1)}, u32[]{:S(2)}) copy-start(pred[3]{0:T(512)(128)(4,1)} %compare_and_fusion.6) | copy-start | bytes 13
  56.6 5.3 %copy-start.29 = (pred[3]{0:T(512)(128)(4,1)S(1)}, pred[3]{0:T(512)(128)(4,1)}, u32[]{:S(2)}) copy-start(pred[3]{0:T(512)(128)(4,1)} %compare_and_fusion.1) | copy-start | bytes 13
  57.2 4.8 %copy-start.28 = (pred[3]{0:T(512)(128)(4,1)S(1)}, pred[3]{0:T(512)(128)(4,1)}, u32[]{:S(2)}) copy-start(pred[3]{0:T(512)(128)(4,1)} %compare_and_fusion.2) | copy-start | bytes 13
  57.9 4.3 %copy-start.27 = (pred[3]{0:T(512)(128)(4,1)S(1)}, pred[3]{0:T(512)(128)(4,1)}, u32[]{:S(2)}) copy-start(pred[3]{0:T(512)(128)(4,1)} %compare_and_fusion.3) | copy-start | bytes 13
  58.2 5.5 %copy-start = (bf16[1,8,8,1536]{3,2,1,0:T(8,128)(2,1)S(1)}, bf16[1,8,8,1536]{3,2,1,0:T(8,128)(2,1)}, u32[]{:S(2)}) copy-start(bf16[1,8,8,1536]{3,2,1,0:T(8,128)(2,1)} %param.16) | copy-start | bytes 589828
  58.2 5.4 %copy-start.5 = (bf16[1,8,8,1536]{3,2,1,0:T(8,128)(2,1)S(1)}, bf16[1,8,8,1536]{3,2,1,0:T(8,128)(2,1)}, u32[]{:S(2)}) copy-start(bf16[1,8,8,1536]{3,2,1,0:T(8,128)(2,1)} %param.15) | copy-start | bytes 589828
  58.3 6.7 %copy-start.26 = (pred[3]{0:T(512)(128)(4,1)S(1)}, pred[3]{0:T(512)(128)(4,1)}, u32[]{:S(2)}) copy-start(pred[3]{0:T(512)(128)(4,1)} %compare_and_fusion.4) | copy-start | bytes 13
  58.3 16.1 %collective-permute-start = (bf16[3,3,2,128,128]{4,3,2,1,0:T(8,128)(2,1)S(1)}, bf16[3,3,2,128,128]{4,3,2,1,0:T(8,128)(2,1)S(1)}, u32[]{:S(2)}, u32[]{:S(2)}) collective-permute-start(bf16[3,3,2,128,128]{4,3,2,1,0:T(8,128)(2,1)S(1)} %pad_maximum_fusion.4), channel_id=1, source_target_pairs={{0,8},{8,16},{16,24},{1,9},{9,17},{17,25},{2,10},{10,18},{18,26},{... | collective-permute-start | bytes 1769480 | tf_op jit(solution)/shard_map/ppermute | solution.py:12
  62.3 16.6 %collective-permute-start.1 = (bf16[3,3,2,128,128]{4,3,2,1,0:T(8,128)(2,1)S(1)}, bf16[3,3,2,128,128]{4,3,2,1,0:T(8,128)(2,1)S(1)}, u32[]{:S(2)}, u32[]{:S(2)}) collective-permute-start(bf16[3,3,2,128,128]{4,3,2,1,0:T(8,128)(2,1)S(1)} %pad_maximum_fusion.5), channel_id=1, source_target_pairs={{8,0},{16,8},{24,16},{9,1},{17,9},{25,17},{10,2},{18,10},{26,18},{... | collective-permute-start | bytes 1769480 | tf_op jit(solution)/shard_map/ppermute | solution.py:12
  64.4 16.5 %copy-start.15 = (s32[24]{0:T(128)S(1)}, s32[24]{0:T(128)}, u32[]{:S(2)}) copy-start(s32[24]{0:T(128)} %reshape.632) | copy-start | bytes 292
  78.9 2.8 %copy-start.1 = (bf16[3,3,2,128,128]{4,3,2,1,0:T(8,128)(2,1)}, bf16[3,3,2,128,128]{4,3,2,1,0:T(8,128)(2,1)S(1)}, u32[]{:S(2)}) copy-start(bf16[3,3,2,128,128]{4,3,2,1,0:T(8,128)(2,1)S(1)} %collective-permute-done.1) | copy-start | bytes 1769476
  79.0 11.2 %collective-permute-start.2 = (bf16[3,3,2,128,128]{4,3,2,1,0:T(8,128)(2,1)S(1)}, bf16[3,3,2,128,128]{4,3,2,1,0:T(8,128)(2,1)S(1)}, u32[]{:S(2)}, u32[]{:S(2)}) collective-permute-start(bf16[3,3,2,128,128]{4,3,2,1,0:T(8,128)(2,1)S(1)} %pad_maximum_fusion.6), channel_id=1, source_target_pairs={{0,2},{2,4},{4,6},{1,3},{3,5},{5,7},{8,10},{10,12},{12,14},{9,11},... | collective-permute-start | bytes 1769480 | tf_op jit(solution)/shard_map/ppermute | solution.py:12
  81.0 1.5 copy-start.33
  81.0 2.2 copy-start.25
  82.6 15.3 %copy-start.22 = (s32[3]{0:T(128)S(1)}, s32[3]{0:T(128)}, u32[]{:S(2)}) copy-start(s32[3]{0:T(128)} %get-tuple-element.130) | copy-start | bytes 40
  82.6 15.3 %copy-start.24 = (s32[3]{0:T(128)S(1)}, s32[3]{0:T(128)}, u32[]{:S(2)}) copy-start(s32[3]{0:T(128)} %copy-done.23) | copy-start | bytes 40
  90.2 7.6 %copy-start.2 = (bf16[3,3,2,128,128]{4,3,2,1,0:T(8,128)(2,1)}, bf16[3,3,2,128,128]{4,3,2,1,0:T(8,128)(2,1)S(1)}, u32[]{:S(2)}) copy-start(bf16[3,3,2,128,128]{4,3,2,1,0:T(8,128)(2,1)S(1)} %collective-permute-done.2) | copy-start | bytes 1769476
  92.5 52.7 %collective-permute-start.3 = (bf16[3,3,2,128,128]{4,3,2,1,0:T(8,128)(2,1)}, bf16[3,3,2,128,128]{4,3,2,1,0:T(8,128)(2,1)}, u32[]{:S(2)}, u32[]{:S(2)}) collective-permute-start(bf16[3,3,2,128,128]{4,3,2,1,0:T(8,128)(2,1)} %pad_maximum_fusion.7), channel_id=1, source_target_pairs={{2,0},{4,2},{6,4},{3,1},{5,3},{7,5},{10,8},{12,10},{14,12},{11,9},... | collective-permute-start | bytes 1769480 | tf_op jit(solution)/shard_map/ppermute | solution.py:12
  94.4 3.4 %copy-start.7 = (f32[2,1,384]{2,1,0:T(1,128)}, f32[2,1,384]{2,1,0:T(1,128)S(1)}, u32[]{:S(2)}) copy-start(f32[2,1,384]{2,1,0:T(1,128)S(1)} %all-to-all-done.3) | copy-start | bytes 9220
  94.5 11.3 %all-to-all-start.5 = ((f32[2,1,384]{2,1,0:T(1,128)}), f32[2,1,384]{2,1,0:T(1,128)S(1)}, u32[]{:S(2)}, u32[]{:S(2)}) async-start(f32[2,1,384]{2,1,0:T(1,128)} %reshape.759), calls=%async_computation.5 | async-start | bytes 6144 | tf_op jit(solution)/shard_map/all_to_all | solution.py:113
  105.8 8.5 %copy-start.8 = (f32[2,1,384]{2,1,0:T(1,128)}, f32[2,1,384]{2,1,0:T(1,128)S(1)}, u32[]{:S(2)}) copy-start(f32[2,1,384]{2,1,0:T(1,128)S(1)} %all-to-all-done.5) | copy-start | bytes 9220
  105.8 12.8 %all-to-all-start = ((bf16[2,2,24576]{2,1,0:T(2,128)(2,1)}), bf16[2,2,24576]{2,1,0:T(2,128)(2,1)}, u32[]{:S(2)}, u32[]{:S(2)}) async-start(bf16[2,2,24576]{2,1,0:T(2,128)(2,1)} %reshape.749), calls=%async_computation | async-start | bytes 393216 | tf_op jit(solution)/shard_map/all_to_all | solution.py:106
  114.3 9.6 %copy-start.14 = (s32[6,4,1]{0,1,2:T(4,128)S(1)}, s32[6,4,1]{0,1,2:T(4,128)}, u32[]{:S(2)}) copy-start(s32[6,4,1]{0,1,2:T(4,128)} %fusion.43) | copy-start | bytes 292
  118.6 18.5 %all-to-all-start.4 = ((bf16[2,2,24576]{2,1,0:T(2,128)(2,1)}), bf16[2,2,24576]{2,1,0:T(2,128)(2,1)}, u32[]{:S(2)}, u32[]{:S(2)}) async-start(bf16[2,2,24576]{2,1,0:T(2,128)(2,1)} %reshape.757), calls=%async_computation.4 | async-start | bytes 393216 | tf_op jit(solution)/shard_map/all_to_all | solution.py:109
  157.3 0.9 copy-start.6
  190.5 0.6 copy-start.11
  190.5 1.2 copy-start.12
  190.5 1.8 copy-start.13
  191.1 4.5 %copy-start.9 = (s32[3]{0:T(128)S(1)}, s32[3]{0:T(128)}, u32[]{:S(2)}) copy-start(s32[3]{0:T(128)} %fusion.86) | copy-start | bytes 40
  191.1 5.1 %copy-start.10 = (s32[3]{0:T(128)S(1)}, s32[3]{0:T(128)}, u32[]{:S(2)}) copy-start(s32[3]{0:T(128)} %fusion.87) | copy-start | bytes 40
  193.0 10.7 %collective-permute-start.4 = (bf16[3,3,2,128,128]{4,3,2,1,0:T(8,128)(2,1)S(1)}, bf16[3,3,2,128,128]{4,3,2,1,0:T(8,128)(2,1)S(1)}, u32[]{:S(2)}, u32[]{:S(2)}) collective-permute-start(bf16[3,3,2,128,128]{4,3,2,1,0:T(8,128)(2,1)S(1)} %pad_maximum_fusion.8), channel_id=1, source_target_pairs={{2,0},{4,2},{6,4},{3,1},{5,3},{7,5},{10,8},{12,10},{14,12},{11,9},... | collective-permute-start | bytes 1769480 | tf_op jit(solution)/shard_map/ppermute | solution.py:12
  198.3 11.5 %collective-permute-start.5 = (bf16[3,3,2,128,128]{4,3,2,1,0:T(8,128)(2,1)}, bf16[3,3,2,128,128]{4,3,2,1,0:T(8,128)(2,1)}, u32[]{:S(2)}, u32[]{:S(2)}) collective-permute-start(bf16[3,3,2,128,128]{4,3,2,1,0:T(8,128)(2,1)} %pad_maximum_fusion.9), channel_id=1, source_target_pairs={{0,2},{2,4},{4,6},{1,3},{3,5},{5,7},{8,10},{10,12},{12,14},{9,11},... | collective-permute-start | bytes 1769480 | tf_op jit(solution)/shard_map/ppermute | solution.py:12
  211.0 10.8 %collective-permute-start.7 = (bf16[3,3,2,128,128]{4,3,2,1,0:T(8,128)(2,1)S(1)}, bf16[3,3,2,128,128]{4,3,2,1,0:T(8,128)(2,1)S(1)}, u32[]{:S(2)}, u32[]{:S(2)}) collective-permute-start(bf16[3,3,2,128,128]{4,3,2,1,0:T(8,128)(2,1)S(1)} %pad_maximum_fusion.11), channel_id=1, source_target_pairs={{0,8},{8,16},{16,24},{1,9},{9,17},{17,25},{2,10},{10,18},{18,26},{... | collective-permute-start | bytes 1769480 | tf_op jit(solution)/shard_map/ppermute | solution.py:12
  214.6 11.9 %collective-permute-start.6 = (bf16[3,3,2,128,128]{4,3,2,1,0:T(8,128)(2,1)S(1)}, bf16[3,3,2,128,128]{4,3,2,1,0:T(8,128)(2,1)}, u32[]{:S(2)}, u32[]{:S(2)}) collective-permute-start(bf16[3,3,2,128,128]{4,3,2,1,0:T(8,128)(2,1)S(1)} %pad_maximum_fusion.10), channel_id=1, source_target_pairs={{8,0},{16,8},{24,16},{9,1},{17,9},{25,17},{10,2},{18,10},{26,18},{... | collective-permute-start | bytes 1769480 | tf_op jit(solution)/shard_map/ppermute | solution.py:12
  217.0 14.4 %all-to-all-start.6 = ((bf16[2,8,8,768]{3,2,1,0:T(8,128)(2,1)}), bf16[2,8,8,768]{3,2,1,0:T(8,128)(2,1)S(1)}, u32[]{:S(2)}, u32[]{:S(2)}) async-start(bf16[2,8,8,768]{3,2,1,0:T(8,128)(2,1)} %reshape.555), calls=%async_computation.6 | async-start | bytes 393216 | tf_op jit(solution)/shard_map/all_to_all | solution.py:206
  221.9 4.6 %copy-start.3 = (bf16[3,3,2,128,128]{4,3,2,1,0:T(8,128)(2,1)}, bf16[3,3,2,128,128]{4,3,2,1,0:T(8,128)(2,1)S(1)}, u32[]{:S(2)}) copy-start(bf16[3,3,2,128,128]{4,3,2,1,0:T(8,128)(2,1)S(1)} %collective-permute-done.7) | copy-start | bytes 1769476
  231.4 8.2 %all-to-all-start.8 = ((bf16[2,8,8,768]{3,2,1,0:T(8,128)(2,1)}), bf16[2,8,8,768]{3,2,1,0:T(8,128)(2,1)S(1)}, u32[]{:S(2)}, u32[]{:S(2)}) async-start(bf16[2,8,8,768]{3,2,1,0:T(8,128)(2,1)} %reshape.557), calls=%async_computation.8 | async-start | bytes 393216 | tf_op jit(solution)/shard_map/all_to_all | solution.py:208
  239.7 8.2 %all-to-all-start.7 = ((bf16[2,8,8,768]{3,2,1,0:T(8,128)(2,1)}), bf16[2,8,8,768]{3,2,1,0:T(8,128)(2,1)S(1)}, u32[]{:S(2)}, u32[]{:S(2)}) async-start(bf16[2,8,8,768]{3,2,1,0:T(8,128)(2,1)} %reshape.556), calls=%async_computation.7 | async-start | bytes 393216 | tf_op jit(solution)/shard_map/all_to_all | solution.py:207
where the time goes:
time: 252 us; the launch traced here: 249 us
  local copies, waits for them, and re-layouts  107 us (42%)
  starting transfers between devices  51 us (20%)
  waiting for transfers between devices  40.1 us (16%)
  matrix products  24.6 us (10%)
  other arithmetic  24.4 us (10%)
    unnamed x101, local copies, waits for them, and re-layouts  58.1 us
    ppermute x8, waiting for transfers between devices, passed_along(): return lax.ppermute(block, axis, route)  32.9 us
    ppermute x8, starting transfers between devices, passed_along(): return lax.ppermute(block, axis, route)  18.3 us
    dot_general x6, matrix products, query_side(): lax.dot_general(score_bf, q_rows, contract_rows, preferred_element_type=j...  10.3 us
    concatenate x8, other arithmetic, local(): part_bf[head_of[direction], place_of[direction]]  6.04 us
    dot_general x6, matrix products, query_side(): lax.dot_general(q_rows, k_rows, contract_cols, preferred_element_type=jnp...  5.93 us
    dot_general x6, matrix products, query_side(): lax.dot_general(prob_bf, g_rows, contract_rows, preferred_element_type=jn...  5.82 us
    gather x8, local copies, waits for them, and re-layouts, local(): jnp.take(kv_own, head_of[direction], axis=0)  5.17 us
  transfers between devices with their start and end apart: 17, of which 8 were waited for; matrix products, arithmetic and copies ran while one was open for 40% of the time, Pallas kernels for 0%

commit v1 on v0

--- a/solution.py
+++ b/solution.py
@@ -105,7 +105,10 @@
     q_heads, k_heads, v_heads, g_heads = (
         lax.all_to_all(queries, "tp", split_axis=3, concat_axis=0, tiled=True),
         lax.all_to_all(keys, "tp", split_axis=3, concat_axis=0, tiled=True),
-        lax.all_to_all(values, "tp", split_axis=3, concat_axis=0, tiled=True),
+        jnp.concatenate(
+            lax.all_to_all(jnp.stack(jnp.split(values, lax.axis_size("tp"), axis=3)), "tp", 0, 0),
+            axis=0,
+        ),
         lax.all_to_all(attn_grad, "tp", split_axis=3, concat_axis=0, tiled=True),
     )
     lse_heads, delta_heads = (

time: 252 us -> 242 us (0.960)
  local copies, waits for them, and re-layouts: 107 us -> 91.6 us
  other arithmetic: 24.4 us -> 27.8 us
  waiting for transfers between devices: 40.1 us -> 42.9 us
    unnamed x101 -> x94, local copies, waits for them, and re-layouts: 58.1 us -> 46.4 us
    all_to_all x1, waiting for transfers between devices: 0.01 us -> 3.92 us  [local(): lax.all_to_all(keys, 'tp', split_axis=3, concat_axis=0, tiled=True)]
  transfers between devices with their start and end apart: 17 -> 17, of which waited for: 8 -> 9; matrix products, arithmetic and copies ran while one was open for 40% -> 39% of each run, Pallas kernels for 0% -> 0%
where the time goes in v1:
time: 242 us; the launch traced here: 239 us
  local copies, waits for them, and re-layouts  91.6 us (38%)
  starting transfers between devices  50.6 us (21%)
  waiting for transfers between devices  42.9 us (18%)
  other arithmetic  27.8 us (11%)
  matrix products  24.6 us (10%)
    unnamed x94, local copies, waits for them, and re-layouts  46.4 us
    ppermute x8, waiting for transfers between devices, passed_along(): return lax.ppermute(block, axis, route)  31.8 us
    ppermute x8, starting transfers between devices, passed_along(): return lax.ppermute(block, axis, route)  18.1 us
    dot_general x6, matrix products, query_side(): lax.dot_general(score_bf, q_rows, contract_rows, preferred_element_type=j...  10.3 us
    concatenate x8, other arithmetic, local(): part_bf[head_of[direction], place_of[direction]]  6.04 us
    dot_general x6, matrix products, query_side(): lax.dot_general(q_rows, k_rows, contract_cols, preferred_element_type=jnp...  5.94 us
    dot_general x6, matrix products, query_side(): lax.dot_general(prob_bf, g_rows, contract_rows, preferred_element_type=jn...  5.82 us
    gather x8, local copies, waits for them, and re-layouts, local(): jnp.take(kv_own, head_of[direction], axis=0)  5.66 us
  transfers between devices with their start and end apart: 17, of which 9 were waited for; matrix products, arithmetic and copies ran while one was open for 39% of the time, Pallas kernels for 0%

profile of v1, /device:TPU:4, one launch (start us, length us, event | category | flops | bytes accessed | tf_op | source)
XLA Modules:
  0.0 239.3 jit_solution(3162273360823972988)
XLA Ops:
  0.6 1.0 slice_bitcast_fusion.5
  2.3 3.4 %all-to-all-start.2 = ((bf16[2,1,8,8,768]{4,3,2,1,0:T(8,128)(2,1)}), bf16[2,1,8,8,768]{4,3,2,1,0:T(8,128)(2,1)S(1)}, u32[]{:S(2)}, u32[]{:S(2)}) async-start(bf16[2,1,8,8,768]{4,3,2,1,0:T(8,128)(2,1)} %pad_maximum_fusion.13), calls=%async_computation.2 | async-start | bytes 393216 | tf_op jit(solution)/shard_map/all_to_all | solution.py:109
  20.6 2.2 copy.101
  22.9 4.1 %reshape.746 = bf16[2,2,24576]{2,1,0:T(2,128)(2,1)} reshape(bf16[1536,1,8,8]{3,2,1,0:T(8,128)(2,1)S(1)} %bitcast.298) | data formatting | bytes 393216
  27.6 3.4 %all-to-all-start.1 = ((bf16[2,2,24576]{2,1,0:T(2,128)(2,1)}), bf16[2,2,24576]{2,1,0:T(2,128)(2,1)S(1)}, u32[]{:S(2)}, u32[]{:S(2)}) async-start(bf16[2,2,24576]{2,1,0:T(2,128)(2,1)} %reshape.746), calls=%async_computation.1 | async-start | bytes 393216 | tf_op jit(solution)/shard_map/all_to_all | solution.py:107
  31.9 3.9 %all-to-all-done.1 = bf16[2,2,24576]{2,1,0:T(2,128)(2,1)S(1)} async-done(((bf16[2,2,24576]{2,1,0:T(2,128)(2,1)}), bf16[2,2,24576]{2,1,0:T(2,128)(2,1)S(1)}, u32[]{:S(2)}, u32[]{:S(2)}) %all-to-all-start.1) | async-done | bytes 196640 | tf_op jit(solution)/shard_map/all_to_all | solution.py:107
  35.8 3.8 %all-to-all-start.3 = ((f32[2,1,384]{2,1,0:T(1,128)}), f32[2,1,384]{2,1,0:T(1,128)}, u32[]{:S(2)}, u32[]{:S(2)}) async-start(f32[2,1,384]{2,1,0:T(1,128)} %reshape.748), calls=%async_computation.3 | async-start | bytes 6144 | tf_op jit(solution)/shard_map/all_to_all | solution.py:115
  39.6 3.7 %reshape.747 = bf16[1536,1,8,8]{3,2,1,0:T(8,128)(2,1)S(1)} reshape(bf16[2,2,24576]{2,1,0:T(2,128)(2,1)S(1)} %all-to-all-done.1) | data formatting | bytes 393216
  43.3 1.6 copy.102
  50.0 3.6 %collective-permute-start = (bf16[3,3,2,128,128]{4,3,2,1,0:T(8,128)(2,1)S(1)}, bf16[3,3,2,128,128]{4,3,2,1,0:T(8,128)(2,1)S(1)}, u32[]{:S(2)}, u32[]{:S(2)}) collective-permute-start(bf16[3,3,2,128,128]{4,3,2,1,0:T(8,128)(2,1)S(1)} %pad_maximum_fusion.4), channel_id=1, source_target_pairs={{0,8},{8,16},{16,24},{1,9},{9,17},{17,25},{2,10},{10,18},{18,26},{... | collective-permute-start | bytes 1769480 | tf_op jit(solution)/shard_map/ppermute | solution.py:12
  54.1 1.3 collective-permute-start.1
  57.1 8.0 %collective-permute-done = bf16[3,3,2,128,128]{4,3,2,1,0:T(8,128)(2,1)S(1)} collective-permute-done((bf16[3,3,2,128,128]{4,3,2,1,0:T(8,128)(2,1)S(1)}, bf16[3,3,2,128,128]{4,3,2,1,0:T(8,128)(2,1)S(1)}, u32[]{:S(2)}, u32[]{:S(2)}) %collective-permute-start) | collective-permute-done | bytes 589856 | tf_op jit(solution)/shard_map/ppermute | solution.py:12
  65.1 4.5 %collective-permute-done.1 = bf16[3,3,2,128,128]{4,3,2,1,0:T(8,128)(2,1)S(1)} collective-permute-done((bf16[3,3,2,128,128]{4,3,2,1,0:T(8,128)(2,1)S(1)}, bf16[3,3,2,128,128]{4,3,2,1,0:T(8,128)(2,1)S(1)}, u32[]{:S(2)}, u32[]{:S(2)}) %collective-permute-start.1) | collective-permute-done | bytes 589856 | tf_op jit(solution)/shard_map/ppermute | solution.py:12
  69.7 1.9 collective-permute-start.2
  73.9 7.0 %collective-permute-done.2 = bf16[3,3,2,128,128]{4,3,2,1,0:T(8,128)(2,1)S(1)} collective-permute-done((bf16[3,3,2,128,128]{4,3,2,1,0:T(8,128)(2,1)S(1)}, bf16[3,3,2,128,128]{4,3,2,1,0:T(8,128)(2,1)S(1)}, u32[]{:S(2)}, u32[]{:S(2)}) %collective-permute-start.2) | collective-permute-done | bytes 589856 | tf_op jit(solution)/shard_map/ppermute | solution.py:12
  83.2 1.9 collective-permute-start.3
  85.1 3.2 %all-to-all-start.5 = ((f32[2,1,384]{2,1,0:T(1,128)}), f32[2,1,384]{2,1,0:T(1,128)S(1)}, u32[]{:S(2)}, u32[]{:S(2)}) async-start(f32[2,1,384]{2,1,0:T(1,128)} %reshape.752), calls=%async_computation.5 | async-start | bytes 6144 | tf_op jit(solution)/shard_map/all_to_all | solution.py:116
  88.9 3.1 %copy.99 = bf16[1,8,8,1536]{2,1,0,3:T(8,128)(2,1)S(1)} copy(bf16[1,8,8,1536]{3,2,1,0:T(8,128)(2,1)} %param.12) | data formatting | bytes 393216 | tf_op args[0]
  92.0 4.2 %reshape.744 = bf16[2,2,24576]{2,1,0:T(2,128)(2,1)} reshape(bf16[1536,1,8,8]{3,2,1,0:T(8,128)(2,1)S(1)} %bitcast.299) | data formatting | bytes 393216
  96.3 4.3 %all-to-all-start = ((bf16[2,2,24576]{2,1,0:T(2,128)(2,1)}), bf16[2,2,24576]{2,1,0:T(2,128)(2,1)}, u32[]{:S(2)}, u32[]{:S(2)}) async-start(bf16[2,2,24576]{2,1,0:T(2,128)(2,1)} %reshape.744), calls=%async_computation | async-start | bytes 393216 | tf_op jit(solution)/shard_map/all_to_all | solution.py:106
  100.5 1.3 fusion.91
  101.8 3.1 %copy.111 = bf16[1,8,8,1536]{2,1,0,3:T(8,128)(2,1)S(1)} copy(bf16[1,8,8,1536]{3,2,1,0:T(8,128)(2,1)} %param.16) | data formatting | bytes 393216 | tf_op args[4]
  105.0 4.2 %reshape.750 = bf16[2,2,24576]{2,1,0:T(2,128)(2,1)} reshape(bf16[1536,1,8,8]{3,2,1,0:T(8,128)(2,1)S(1)} %bitcast.300) | data formatting | bytes 393216
  109.2 4.1 %all-to-all-start.4 = ((bf16[2,2,24576]{2,1,0:T(2,128)(2,1)}), bf16[2,2,24576]{2,1,0:T(2,128)(2,1)}, u32[]{:S(2)}, u32[]{:S(2)}) async-start(bf16[2,2,24576]{2,1,0:T(2,128)(2,1)} %reshape.750), calls=%async_computation.4 | async-start | bytes 393216 | tf_op jit(solution)/shard_map/all_to_all | solution.py:112
  113.3 1.3 fusion.92
  115.9 1.3 reduce.43
  117.4 1.3 reduce.44
  118.9 4.5 %reshape.745 = bf16[1536,1,8,8]{3,2,1,0:T(8,128)(2,1)S(1)} reshape(bf16[2,2,24576]{2,1,0:T(2,128)(2,1)} %all-to-all-done) | data formatting | bytes 393216
  123.5 2.4 copy.100
  125.9 1.2 reshape.541
  127.7 4.5 %reshape.751 = bf16[1536,1,8,8]{3,2,1,0:T(8,128)(2,1)S(1)} reshape(bf16[2,2,24576]{2,1,0:T(2,128)(2,1)} %all-to-all-done.4) | data formatting | bytes 393216
  132.3 2.4 copy.112
  134.6 1.2 reshape.546
  135.9 1.6 slice_dynamic-update-slice_fusion.5
  137.5 1.6 slice_dynamic-update-slice_fusion.4
  139.1 1.6 slice_dynamic-update-slice_fusion.3
  140.7 1.6 slice_dynamic-update-slice_fusion.2
  142.3 1.6 slice_dynamic-update-slice_fusion.1
  143.9 1.6 slice_dynamic-update-slice_fusion
  145.6 2.3 gather_fusion
  148.9 29.2 %while.14 = (s32[]{:T(128)}, bf16[6,128,128]{2,1,0:T(8,128)(2,1)S(1)}, f32[6,640,128]{2,1,0:T(8,128)}, f32[6,640,128]{2,1,0:T(8,128)}, bf16[6,128,128]{2,1,0:T(8...) while((s32[]{:T(128)}, ...), condition=%wide.region_6.8_spmd, body=%wide.region_5.7_spmd.sunk | while | flops 105529344 | bytes 2835589 | solution.py:180
  152.1 1.7 fusion.131
  156.9 1.7 fusion.131
  161.8 1.7 fusion.131
  166.7 1.7 fusion.131
  171.6 1.7 fusion.131
  176.4 1.7 fusion.131
  178.1 1.5 slice.304
  179.7 1.5 slice.305
  183.7 1.9 collective-permute-start.4
  189.0 2.6 %collective-permute-start.5 = (bf16[3,3,2,128,128]{4,3,2,1,0:T(8,128)(2,1)}, bf16[3,3,2,128,128]{4,3,2,1,0:T(8,128)(2,1)}, u32[]{:S(2)}, u32[]{:S(2)}) collective-permute-start(bf16[3,3,2,128,128]{4,3,2,1,0:T(8,128)(2,1)} %pad_maximum_fusion.9), channel_id=1, source_target_pairs={{0,2},{2,4},{4,6},{1,3},{3,5},{5,7},{8,10},{10,12},{12,14},{9,11},... | collective-permute-start | bytes 1769480 | tf_op jit(solution)/shard_map/ppermute | solution.py:12
  194.2 6.3 %collective-permute-done.5 = bf16[3,3,2,128,128]{4,3,2,1,0:T(8,128)(2,1)} collective-permute-done((bf16[3,3,2,128,128]{4,3,2,1,0:T(8,128)(2,1)}, bf16[3,3,2,128,128]{4,3,2,1,0:T(8,128)(2,1)}, u32[]{:S(2)}, u32[]{:S(2)}) %collective-permute-start.5) | collective-permute-done | bytes 589856 | tf_op jit(solution)/shard_map/ppermute | solution.py:12
  200.5 1.2 fusion.94
  201.7 3.5 %collective-permute-start.7 = (bf16[3,3,2,128,128]{4,3,2,1,0:T(8,128)(2,1)S(1)}, bf16[3,3,2,128,128]{4,3,2,1,0:T(8,128)(2,1)S(1)}, u32[]{:S(2)}, u32[]{:S(2)}) collective-permute-start(bf16[3,3,2,128,128]{4,3,2,1,0:T(8,128)(2,1)S(1)} %pad_maximum_fusion.11), channel_id=1, source_target_pairs={{0,8},{8,16},{16,24},{1,9},{9,17},{17,25},{2,10},{10,18},{18,26},{... | collective-permute-start | bytes 1769480 | tf_op jit(solution)/shard_map/ppermute | solution.py:12
  205.3 1.3 collective-permute-start.6
  207.6 3.4 %all-to-all-start.6 = ((bf16[2,8,8,768]{3,2,1,0:T(8,128)(2,1)}), bf16[2,8,8,768]{3,2,1,0:T(8,128)(2,1)S(1)}, u32[]{:S(2)}, u32[]{:S(2)}) async-start(bf16[2,8,8,768]{3,2,1,0:T(8,128)(2,1)} %reshape.550), calls=%async_computation.6 | async-start | bytes 393216 | tf_op jit(solution)/shard_map/all_to_all | solution.py:209
  211.1 1.5 collective-permute-done.7
  212.5 4.6 %collective-permute-done.6 = bf16[3,3,2,128,128]{4,3,2,1,0:T(8,128)(2,1)} collective-permute-done((bf16[3,3,2,128,128]{4,3,2,1,0:T(8,128)(2,1)S(1)}, bf16[3,3,2,128,128]{4,3,2,1,0:T(8,128)(2,1)}, u32[]{:S(2)}, u32[]{:S(2)}) %collective-permute-start.6) | collective-permute-done | bytes 589856 | tf_op jit(solution)/shard_map/ppermute | solution.py:12
  217.2 1.4 pad_maximum_fusion.1
  219.8 1.2 fusion.38
  222.1 3.4 %all-to-all-start.8 = ((bf16[2,8,8,768]{3,2,1,0:T(8,128)(2,1)}), bf16[2,8,8,768]{3,2,1,0:T(8,128)(2,1)S(1)}, u32[]{:S(2)}, u32[]{:S(2)}) async-start(bf16[2,8,8,768]{3,2,1,0:T(8,128)(2,1)} %reshape.552), calls=%async_computation.8 | async-start | bytes 393216 | tf_op jit(solution)/shard_map/all_to_all | solution.py:211
  226.6 3.7 %all-to-all-done.8 = bf16[2,8,8,768]{3,2,1,0:T(8,128)(2,1)S(1)} async-done(((bf16[2,8,8,768]{3,2,1,0:T(8,128)(2,1)}), bf16[2,8,8,768]{3,2,1,0:T(8,128)(2,1)S(1)}, u32[]{:S(2)}, u32[]{:S(2)}) %all-to-all-start.8) | async-done | bytes 196640 | tf_op jit(solution)/shard_map/all_to_all | solution.py:211
  230.3 3.4 %all-to-all-start.7 = ((bf16[2,8,8,768]{3,2,1,0:T(8,128)(2,1)}), bf16[2,8,8,768]{3,2,1,0:T(8,128)(2,1)S(1)}, u32[]{:S(2)}, u32[]{:S(2)}) async-start(bf16[2,8,8,768]{3,2,1,0:T(8,128)(2,1)} %reshape.551), calls=%async_computation.7 | async-start | bytes 393216 | tf_op jit(solution)/shard_map/all_to_all | solution.py:210
  235.1 3.4 %all-to-all-done.7 = bf16[2,8,8,768]{3,2,1,0:T(8,128)(2,1)S(1)} async-done(((bf16[2,8,8,768]{3,2,1,0:T(8,128)(2,1)}), bf16[2,8,8,768]{3,2,1,0:T(8,128)(2,1)S(1)}, u32[]{:S(2)}, u32[]{:S(2)}) %all-to-all-start.7) | async-done | bytes 196640 | tf_op jit(solution)/shard_map/all_to_all | solution.py:210
  (242 shorter events, 66.1 us)
Async XLA Ops:
  0.6 20.0 %copy-start.4 = (bf16[1,8,8,1536]{3,2,1,0:T(8,128)(2,1)S(1)}, bf16[1,8,8,1536]{3,2,1,0:T(8,128)(2,1)}, u32[]{:S(2)}) copy-start(bf16[1,8,8,1536]{3,2,1,0:T(8,128)(2,1)} %param.13) | copy-start | bytes 589828
  2.3 25.2 %all-to-all-start.2 = ((bf16[2,1,8,8,768]{4,3,2,1,0:T(8,128)(2,1)}), bf16[2,1,8,8,768]{4,3,2,1,0:T(8,128)(2,1)S(1)}, u32[]{:S(2)}, u32[]{:S(2)}) async-start(bf16[2,1,8,8,768]{4,3,2,1,0:T(8,128)(2,1)} %pad_maximum_fusion.13), calls=%async_computation.2 | async-start | bytes 393216 | tf_op jit(solution)/shard_map/all_to_all | solution.py:109
  8.0 6.2 %copy-start.15 = (s32[3]{0:T(128)}, s32[3]{0:T(128)S(1)}, u32[]{:S(2)}) copy-start(s32[3]{0:T(128)S(1)} %get-tuple-element.188) | copy-start | bytes 40
  8.0 10.5 %copy-start.16 = (s32[3]{0:T(128)}, s32[3]{0:T(128)S(1)}, u32[]{:S(2)}) copy-start(s32[3]{0:T(128)S(1)} %get-tuple-element.184) | copy-start | bytes 40
  8.0 10.5 %copy-start.17 = (s32[3]{0:T(128)}, s32[3]{0:T(128)S(1)}, u32[]{:S(2)}) copy-start(s32[3]{0:T(128)S(1)} %get-tuple-element.185) | copy-start | bytes 40
  8.0 10.5 %copy-start.18 = (s32[3]{0:T(128)}, s32[3]{0:T(128)S(1)}, u32[]{:S(2)}) copy-start(s32[3]{0:T(128)S(1)} %get-tuple-element.183) | copy-start | bytes 40
  8.0 10.5 %copy-start.19 = (s32[3]{0:T(128)}, s32[3]{0:T(128)S(1)}, u32[]{:S(2)}) copy-start(s32[3]{0:T(128)S(1)} %get-tuple-element.186) | copy-start | bytes 40
  8.0 10.5 %copy-start.21 = (s32[3]{0:T(128)}, s32[3]{0:T(128)S(1)}, u32[]{:S(2)}) copy-start(s32[3]{0:T(128)S(1)} %get-tuple-element.187) | copy-start | bytes 40
  22.8 4.1 %copy-start.32 = (s32[8,1]{0,1:T(1,128)S(1)}, s32[8,1]{0,1:T(1,128)}, u32[]{:S(2)}) copy-start(s32[8,1]{0,1:T(1,128)} %constant.90) | copy-start | bytes 100
  22.9 4.1 %copy-start.33 = (s32[8,1]{0,1:T(1,128)S(1)}, s32[8,1]{0,1:T(1,128)}, u32[]{:S(2)}) copy-start(s32[8,1]{0,1:T(1,128)} %constant.89) | copy-start | bytes 100
  22.9 4.1 %copy-start.35 = (s32[3]{0:T(128)S(1)}, s32[3]{0:T(128)}, u32[]{:S(2)}) copy-start(s32[3]{0:T(128)} %compare_select_fusion.8) | copy-start | bytes 40
  22.9 8.1 %copy-start.34 = (s32[3]{0:T(128)S(1)}, s32[3]{0:T(128)}, u32[]{:S(2)}) copy-start(s32[3]{0:T(128)} %compare_select_fusion.9) | copy-start | bytes 40
  27.6 8.2 %all-to-all-start.1 = ((bf16[2,2,24576]{2,1,0:T(2,128)(2,1)}), bf16[2,2,24576]{2,1,0:T(2,128)(2,1)S(1)}, u32[]{:S(2)}, u32[]{:S(2)}) async-start(bf16[2,2,24576]{2,1,0:T(2,128)(2,1)} %reshape.746), calls=%async_computation.1 | async-start | bytes 393216 | tf_op jit(solution)/shard_map/all_to_all | solution.py:107
  35.8 49.3 %all-to-all-start.3 = ((f32[2,1,384]{2,1,0:T(1,128)}), f32[2,1,384]{2,1,0:T(1,128)}, u32[]{:S(2)}, u32[]{:S(2)}) async-start(f32[2,1,384]{2,1,0:T(1,128)} %reshape.748), calls=%async_computation.3 | async-start | bytes 6144 | tf_op jit(solution)/shard_map/all_to_all | solution.py:115
  45.2 4.4 %copy-start.30 = (pred[3]{0:T(512)(128)(4,1)S(1)}, pred[3]{0:T(512)(128)(4,1)}, u32[]{:S(2)}) copy-start(pred[3]{0:T(512)(128)(4,1)} %compare_and_fusion.5) | copy-start | bytes 13
  45.3 4.4 %copy-start.29 = (pred[3]{0:T(512)(128)(4,1)S(1)}, pred[3]{0:T(512)(128)(4,1)}, u32[]{:S(2)}) copy-start(pred[3]{0:T(512)(128)(4,1)} %compare_and_fusion.7) | copy-start | bytes 13
  45.3 4.5 %copy-start.28 = (pred[3]{0:T(512)(128)(4,1)S(1)}, pred[3]{0:T(512)(128)(4,1)}, u32[]{:S(2)}) copy-start(pred[3]{0:T(512)(128)(4,1)} %compare_and_fusion.6) | copy-start | bytes 13
  48.1 5.5 %copy-start.27 = (pred[3]{0:T(512)(128)(4,1)S(1)}, pred[3]{0:T(512)(128)(4,1)}, u32[]{:S(2)}) copy-start(pred[3]{0:T(512)(128)(4,1)} %compare_and_fusion.1) | copy-start | bytes 13
  48.9 4.9 %copy-start.26 = (pred[3]{0:T(512)(128)(4,1)S(1)}, pred[3]{0:T(512)(128)(4,1)}, u32[]{:S(2)}) copy-start(pred[3]{0:T(512)(128)(4,1)} %compare_and_fusion.2) | copy-start | bytes 13
  49.6 4.3 %copy-start.25 = (pred[3]{0:T(512)(128)(4,1)S(1)}, pred[3]{0:T(512)(128)(4,1)}, u32[]{:S(2)}) copy-start(pred[3]{0:T(512)(128)(4,1)} %compare_and_fusion.3) | copy-start | bytes 13
  49.9 5.5 %copy-start = (bf16[1,8,8,1536]{3,2,1,0:T(8,128)(2,1)S(1)}, bf16[1,8,8,1536]{3,2,1,0:T(8,128)(2,1)}, u32[]{:S(2)}) copy-start(bf16[1,8,8,1536]{3,2,1,0:T(8,128)(2,1)} %param.16) | copy-start | bytes 589828
  49.9 5.5 %copy-start.5 = (bf16[1,8,8,1536]{3,2,1,0:T(8,128)(2,1)S(1)}, bf16[1,8,8,1536]{3,2,1,0:T(8,128)(2,1)}, u32[]{:S(2)}) copy-start(bf16[1,8,8,1536]{3,2,1,0:T(8,128)(2,1)} %param.15) | copy-start | bytes 589828
  50.0 7.0 %copy-start.24 = (pred[3]{0:T(512)(128)(4,1)S(1)}, pred[3]{0:T(512)(128)(4,1)}, u32[]{:S(2)}) copy-start(pred[3]{0:T(512)(128)(4,1)} %compare_and_fusion.4) | copy-start | bytes 13
  50.0 15.0 %collective-permute-start = (bf16[3,3,2,128,128]{4,3,2,1,0:T(8,128)(2,1)S(1)}, bf16[3,3,2,128,128]{4,3,2,1,0:T(8,128)(2,1)S(1)}, u32[]{:S(2)}, u32[]{:S(2)}) collective-permute-start(bf16[3,3,2,128,128]{4,3,2,1,0:T(8,128)(2,1)S(1)} %pad_maximum_fusion.4), channel_id=1, source_target_pairs={{0,8},{8,16},{16,24},{1,9},{9,17},{17,25},{2,10},{10,18},{18,26},{... | collective-permute-start | bytes 1769480 | tf_op jit(solution)/shard_map/ppermute | solution.py:12
  54.1 15.5 %collective-permute-start.1 = (bf16[3,3,2,128,128]{4,3,2,1,0:T(8,128)(2,1)S(1)}, bf16[3,3,2,128,128]{4,3,2,1,0:T(8,128)(2,1)S(1)}, u32[]{:S(2)}, u32[]{:S(2)}) collective-permute-start(bf16[3,3,2,128,128]{4,3,2,1,0:T(8,128)(2,1)S(1)} %pad_maximum_fusion.5), channel_id=1, source_target_pairs={{8,0},{16,8},{24,16},{9,1},{17,9},{25,17},{10,2},{18,10},{26,18},{... | collective-permute-start | bytes 1769480 | tf_op jit(solution)/shard_map/ppermute | solution.py:12
  56.2 15.5 %copy-start.14 = (s32[24]{0:T(128)S(1)}, s32[24]{0:T(128)}, u32[]{:S(2)}) copy-start(s32[24]{0:T(128)} %reshape.627) | copy-start | bytes 292
  69.6 2.8 %copy-start.1 = (bf16[3,3,2,128,128]{4,3,2,1,0:T(8,128)(2,1)}, bf16[3,3,2,128,128]{4,3,2,1,0:T(8,128)(2,1)S(1)}, u32[]{:S(2)}) copy-start(bf16[3,3,2,128,128]{4,3,2,1,0:T(8,128)(2,1)S(1)} %collective-permute-done.1) | copy-start | bytes 1769476
  69.7 11.2 %collective-permute-start.2 = (bf16[3,3,2,128,128]{4,3,2,1,0:T(8,128)(2,1)S(1)}, bf16[3,3,2,128,128]{4,3,2,1,0:T(8,128)(2,1)S(1)}, u32[]{:S(2)}, u32[]{:S(2)}) collective-permute-start(bf16[3,3,2,128,128]{4,3,2,1,0:T(8,128)(2,1)S(1)} %pad_maximum_fusion.6), channel_id=1, source_target_pairs={{0,2},{2,4},{4,6},{1,3},{3,5},{5,7},{8,10},{10,12},{12,14},{9,11},... | collective-permute-start | bytes 1769480 | tf_op jit(solution)/shard_map/ppermute | solution.py:12
  71.7 1.5 copy-start.31
  71.7 2.2 copy-start.23
  73.2 15.1 %copy-start.20 = (s32[3]{0:T(128)S(1)}, s32[3]{0:T(128)}, u32[]{:S(2)}) copy-start(s32[3]{0:T(128)} %get-tuple-element.130) | copy-start | bytes 40
  73.2 15.1 %copy-start.22 = (s32[3]{0:T(128)S(1)}, s32[3]{0:T(128)}, u32[]{:S(2)}) copy-start(s32[3]{0:T(128)} %copy-done.21) | copy-start | bytes 40
  80.9 7.5 %copy-start.2 = (bf16[3,3,2,128,128]{4,3,2,1,0:T(8,128)(2,1)}, bf16[3,3,2,128,128]{4,3,2,1,0:T(8,128)(2,1)S(1)}, u32[]{:S(2)}) copy-start(bf16[3,3,2,128,128]{4,3,2,1,0:T(8,128)(2,1)S(1)} %collective-permute-done.2) | copy-start | bytes 1769476
  83.2 52.7 %collective-permute-start.3 = (bf16[3,3,2,128,128]{4,3,2,1,0:T(8,128)(2,1)}, bf16[3,3,2,128,128]{4,3,2,1,0:T(8,128)(2,1)}, u32[]{:S(2)}, u32[]{:S(2)}) collective-permute-start(bf16[3,3,2,128,128]{4,3,2,1,0:T(8,128)(2,1)} %pad_maximum_fusion.7), channel_id=1, source_target_pairs={{2,0},{4,2},{6,4},{3,1},{5,3},{7,5},{10,8},{12,10},{14,12},{11,9},... | collective-permute-start | bytes 1769480 | tf_op jit(solution)/shard_map/ppermute | solution.py:12
  85.1 11.2 %all-to-all-start.5 = ((f32[2,1,384]{2,1,0:T(1,128)}), f32[2,1,384]{2,1,0:T(1,128)S(1)}, u32[]{:S(2)}, u32[]{:S(2)}) async-start(f32[2,1,384]{2,1,0:T(1,128)} %reshape.752), calls=%async_computation.5 | async-start | bytes 6144 | tf_op jit(solution)/shard_map/all_to_all | solution.py:116
  96.3 8.7 %copy-start.7 = (f32[2,1,384]{2,1,0:T(1,128)}, f32[2,1,384]{2,1,0:T(1,128)S(1)}, u32[]{:S(2)}) copy-start(f32[2,1,384]{2,1,0:T(1,128)S(1)} %all-to-all-done.5) | copy-start | bytes 9220
  96.3 12.9 %all-to-all-start = ((bf16[2,2,24576]{2,1,0:T(2,128)(2,1)}), bf16[2,2,24576]{2,1,0:T(2,128)(2,1)}, u32[]{:S(2)}, u32[]{:S(2)}) async-start(bf16[2,2,24576]{2,1,0:T(2,128)(2,1)} %reshape.744), calls=%async_computation | async-start | bytes 393216 | tf_op jit(solution)/shard_map/all_to_all | solution.py:106
  105.0 9.6 %copy-start.13 = (s32[6,4,1]{0,1,2:T(4,128)S(1)}, s32[6,4,1]{0,1,2:T(4,128)}, u32[]{:S(2)}) copy-start(s32[6,4,1]{0,1,2:T(4,128)} %fusion.43) | copy-start | bytes 292
  109.2 18.5 %all-to-all-start.4 = ((bf16[2,2,24576]{2,1,0:T(2,128)(2,1)}), bf16[2,2,24576]{2,1,0:T(2,128)(2,1)}, u32[]{:S(2)}, u32[]{:S(2)}) async-start(bf16[2,2,24576]{2,1,0:T(2,128)(2,1)} %reshape.750), calls=%async_computation.4 | async-start | bytes 393216 | tf_op jit(solution)/shard_map/all_to_all | solution.py:112
  148.0 0.9 copy-start.6
  181.2 0.6 copy-start.10
  181.2 1.2 copy-start.11
  181.2 1.8 copy-start.12
  181.8 4.5 %copy-start.8 = (s32[3]{0:T(128)S(1)}, s32[3]{0:T(128)}, u32[]{:S(2)}) copy-start(s32[3]{0:T(128)} %fusion.86) | copy-start | bytes 40
  181.8 5.1 %copy-start.9 = (s32[3]{0:T(128)S(1)}, s32[3]{0:T(128)}, u32[]{:S(2)}) copy-start(s32[3]{0:T(128)} %fusion.87) | copy-start | bytes 40
  183.7 10.4 %collective-permute-start.4 = (bf16[3,3,2,128,128]{4,3,2,1,0:T(8,128)(2,1)S(1)}, bf16[3,3,2,128,128]{4,3,2,1,0:T(8,128)(2,1)S(1)}, u32[]{:S(2)}, u32[]{:S(2)}) collective-permute-start(bf16[3,3,2,128,128]{4,3,2,1,0:T(8,128)(2,1)S(1)} %pad_maximum_fusion.8), channel_id=1, source_target_pairs={{2,0},{4,2},{6,4},{3,1},{5,3},{7,5},{10,8},{12,10},{14,12},{11,9},... | collective-permute-start | bytes 1769480 | tf_op jit(solution)/shard_map/ppermute | solution.py:12
  189.0 11.5 %collective-permute-start.5 = (bf16[3,3,2,128,128]{4,3,2,1,0:T(8,128)(2,1)}, bf16[3,3,2,128,128]{4,3,2,1,0:T(8,128)(2,1)}, u32[]{:S(2)}, u32[]{:S(2)}) collective-permute-start(bf16[3,3,2,128,128]{4,3,2,1,0:T(8,128)(2,1)} %pad_maximum_fusion.9), channel_id=1, source_target_pairs={{0,2},{2,4},{4,6},{1,3},{3,5},{5,7},{8,10},{10,12},{12,14},{9,11},... | collective-permute-start | bytes 1769480 | tf_op jit(solution)/shard_map/ppermute | solution.py:12
  201.7 10.8 %collective-permute-start.7 = (bf16[3,3,2,128,128]{4,3,2,1,0:T(8,128)(2,1)S(1)}, bf16[3,3,2,128,128]{4,3,2,1,0:T(8,128)(2,1)S(1)}, u32[]{:S(2)}, u32[]{:S(2)}) collective-permute-start(bf16[3,3,2,128,128]{4,3,2,1,0:T(8,128)(2,1)S(1)} %pad_maximum_fusion.11), channel_id=1, source_target_pairs={{0,8},{8,16},{16,24},{1,9},{9,17},{17,25},{2,10},{10,18},{18,26},{... | collective-permute-start | bytes 1769480 | tf_op jit(solution)/shard_map/ppermute | solution.py:12
  205.3 11.9 %collective-permute-start.6 = (bf16[3,3,2,128,128]{4,3,2,1,0:T(8,128)(2,1)S(1)}, bf16[3,3,2,128,128]{4,3,2,1,0:T(8,128)(2,1)}, u32[]{:S(2)}, u32[]{:S(2)}) collective-permute-start(bf16[3,3,2,128,128]{4,3,2,1,0:T(8,128)(2,1)S(1)} %pad_maximum_fusion.10), channel_id=1, source_target_pairs={{8,0},{16,8},{24,16},{9,1},{17,9},{25,17},{10,2},{18,10},{26,18},{... | collective-permute-start | bytes 1769480 | tf_op jit(solution)/shard_map/ppermute | solution.py:12
  207.6 14.4 %all-to-all-start.6 = ((bf16[2,8,8,768]{3,2,1,0:T(8,128)(2,1)}), bf16[2,8,8,768]{3,2,1,0:T(8,128)(2,1)S(1)}, u32[]{:S(2)}, u32[]{:S(2)}) async-start(bf16[2,8,8,768]{3,2,1,0:T(8,128)(2,1)} %reshape.550), calls=%async_computation.6 | async-start | bytes 393216 | tf_op jit(solution)/shard_map/all_to_all | solution.py:209
  212.5 4.6 %copy-start.3 = (bf16[3,3,2,128,128]{4,3,2,1,0:T(8,128)(2,1)}, bf16[3,3,2,128,128]{4,3,2,1,0:T(8,128)(2,1)S(1)}, u32[]{:S(2)}) copy-start(bf16[3,3,2,128,128]{4,3,2,1,0:T(8,128)(2,1)S(1)} %collective-permute-done.7) | copy-start | bytes 1769476
  222.1 8.2 %all-to-all-start.8 = ((bf16[2,8,8,768]{3,2,1,0:T(8,128)(2,1)}), bf16[2,8,8,768]{3,2,1,0:T(8,128)(2,1)S(1)}, u32[]{:S(2)}, u32[]{:S(2)}) async-start(bf16[2,8,8,768]{3,2,1,0:T(8,128)(2,1)} %reshape.552), calls=%async_computation.8 | async-start | bytes 393216 | tf_op jit(solution)/shard_map/all_to_all | solution.py:211
  230.3 8.2 %all-to-all-start.7 = ((bf16[2,8,8,768]{3,2,1,0:T(8,128)(2,1)}), bf16[2,8,8,768]{3,2,1,0:T(8,128)(2,1)S(1)}, u32[]{:S(2)}, u32[]{:S(2)}) async-start(bf16[2,8,8,768]{3,2,1,0:T(8,128)(2,1)} %reshape.551), calls=%async_computation.7 | async-start | bytes 393216 | tf_op jit(solution)/shard_map/all_to_all | solution.py:210
